TPU v7x, 32 devices: a whole 2x2x4 slice. The times are simulated.
32 devices in a mesh: grp: 2 (over y), gx: 16 (over z, x, core).
Axes of the slice: x: 2, y: 2, z: 4, core: 2. Of those that a mesh axis runs over, the one named last changes fastest.
Arguments:
- volume: float32 [512, 896], P(('grp', 'gx')), parts along dimension 0, may hold values from -45 to 45
- bank: float32 [8, 4096], P(None, 'gx'), may hold values from -43 to 43
- orient: int32 [8], replicated, may hold values from 0 to 47
- bank_id: int32 [8], replicated, may hold values from 0 to 7, each once
- counts: int32 [8], replicated, may hold values from 1 to 16
Outputs:
- fields: float32 [4, 512, 896], P(None, ('grp', 'gx')), parts along dimension 1
There are 2 independent parts, one for each index of `grp`. A program takes and returns all parts, laid end to end along the dimension named above; an argument that names none is the same for every part. Nothing has to cross between parts.
Inputs may be any that keep to these rules, and one draw needn't show every extreme that they name: `bank_id`: each of the 8 base templates is named by exactly one list entry.
All inputs are finite; a program needn't handle non-finite values.
Results may differ from a plain program's by a relative error of at most 0.0003.
Values sent between devices are 32-bit elements; how exact they have to be, the bound alone decides.
A program may use at most 64 MiB of HBM per device.

v0:
```python
import math

import jax
import jax.numpy as jnp
import numpy as np
from jax import lax
from jax.sharding import PartitionSpec as P

BY = 8
BZ = 112
TS = 16
NT = 8
FIELDS = 4


epsilon = 1e-05
sharpness = 80.0
AXIS_ORDERS = np.array([[0, 1, 2], [0, 2, 1], [1, 0, 2], [1, 2, 0], [2, 0, 1], [2, 1, 0]], np.int32)


def extended(x, sides, width):
    for axis, dim in sides:
        size, length = (lax.axis_size(axis), x.shape[dim])
        up = [(i, (i + 1) % size) for i in range(size - 1)]
        down = [(j, i) for i, j in up]
        last = lax.slice_in_dim(x, length - width, length, axis=dim)
        leading = lax.slice_in_dim(x, 0, width, axis=dim)
        before = lax.ppermute(last, axis, up)
        after = lax.ppermute(leading, axis, down)
        x = jnp.concatenate([before, x, after], axis=dim)
    return x


def padded_length(length):
    return -(-length // 128) * 128


def rotate_template(flat_base, orient_one):
    coords = jnp.arange(TS**3, dtype=jnp.int32)
    index_set = jnp.stack([coords // (TS * TS), coords // TS % TS, coords % TS])
    order_row = orient_one // 8
    flip_set = orient_one % 8
    picked = (jnp.arange(6, dtype=jnp.int32) == order_row).astype(jnp.int32)
    ordering = jnp.sum(picked[:, None] * jnp.asarray(AXIS_ORDERS), axis=0)
    source = jnp.zeros_like(coords)
    for axis_num in range(3):
        select = (ordering[axis_num] == jnp.arange(3, dtype=jnp.int32)).astype(jnp.int32)
        chosen = jnp.sum(select[:, None] * index_set, axis=0)
        flipped = flip_set // 2**axis_num % 2
        placed = chosen + flipped * (TS - 1 - 2 * chosen)
        source = source * TS + placed
    return flat_base[source]


def normalized_kernel(flat_base, orient_one):
    rotated = rotate_template(flat_base, orient_one)
    centered = rotated - jnp.mean(rotated)
    return centered / jnp.sqrt(jnp.sum(centered * centered) + epsilon)


def wave_tables(positions, targets, period, direction):
    turns = (positions[:, None] * targets[None, :] % period).astype(jnp.float32)
    phase = 2.0 * math.pi / period * turns
    return (jnp.cos(phase), direction * jnp.sin(phase))


def band_table(positions, targets, period):
    offset = (positions[:, None] - targets[None, :]) % period
    return (offset < TS).astype(jnp.float32)


def contract(letters, data, table):
    return jnp.einsum(letters, data, table, precision=lax.Precision.HIGHEST)


def spectrum_along(real_part, imag_part, cos_table, sin_table, letters):
    new_real = contract(letters, real_part, cos_table) - contract(letters, imag_part, sin_table)
    new_imag = contract(letters, real_part, sin_table) + contract(letters, imag_part, cos_table)
    return (new_real, new_imag)


def local(volume, bank, orient, bank_id, counts):
    rows_x = volume.shape[0]
    half = TS // 2
    grid = volume.reshape(rows_x, BY, BZ)
    len_x = rows_x + TS
    len_y = BY + TS
    len_z = padded_length(BZ + TS)
    gathered = lax.all_gather(bank, "gx", axis=1, tiled=True)
    kernels = jax.vmap(normalized_kernel)(gathered[bank_id], orient)
    field_in = extended(grid, (("gx", 0),), half)
    pos_x = jnp.arange(len_x, dtype=jnp.int32)
    out_x = jnp.arange(rows_x, dtype=jnp.int32)
    pos_y = half + jnp.arange(BY, dtype=jnp.int32)
    pos_z = half + jnp.arange(BZ, dtype=jnp.int32)
    freq_x = jnp.arange(len_x, dtype=jnp.int32)
    freq_y = jnp.arange(len_y, dtype=jnp.int32)
    freq_z = jnp.arange(len_z, dtype=jnp.int32)
    tmpl_pos = jnp.arange(TS, dtype=jnp.int32)
    cos_z, sin_z = wave_tables(pos_z, freq_z, len_z, -1.0)
    cos_y, sin_y = wave_tables(pos_y, freq_y, len_y, -1.0)
    cos_x, sin_x = wave_tables(pos_x, freq_x, len_x, -1.0)
    vol_re = contract("xyz,zk->xyk", field_in, cos_z)
    vol_im = contract("xyz,zk->xyk", field_in, sin_z)
    vol_re, vol_im = spectrum_along(vol_re, vol_im, cos_y, sin_y, "xyk,yj->xjk")
    vol_re, vol_im = spectrum_along(vol_re, vol_im, cos_x, sin_x, "xjk,xi->ijk")
    kcos_z, ksin_z = wave_tables(tmpl_pos, freq_z, len_z, -1.0)
    kcos_y, ksin_y = wave_tables(tmpl_pos, freq_y, len_y, -1.0)
    kcos_x, ksin_x = wave_tables(tmpl_pos, freq_x, len_x, -1.0)
    icos_y, isin_y = wave_tables(freq_y, jnp.arange(BY, dtype=jnp.int32), len_y, 1.0)
    icos_x, isin_x = wave_tables(freq_x, out_x, len_x, 1.0)
    icos_z, isin_z = wave_tables(freq_z, jnp.arange(BZ, dtype=jnp.int32), len_z, 1.0)
    inverse_scale = 1.0 / (len_x * len_y * len_z)

    def correlate(kernel_flat):
        kernel = kernel_flat.reshape(TS, TS, TS)
        kernel_re = contract("xyz,zk->xyk", kernel, kcos_z)
        kernel_im = contract("xyz,zk->xyk", kernel, ksin_z)
        kernel_re, kernel_im = spectrum_along(kernel_re, kernel_im, kcos_y, ksin_y, "xyk,yj->xjk")
        kernel_re, kernel_im = spectrum_along(kernel_re, kernel_im, kcos_x, ksin_x, "xjk,xi->ijk")
        prod_re = kernel_re * vol_re + kernel_im * vol_im
        prod_im = kernel_re * vol_im - kernel_im * vol_re
        prod_re, prod_im = spectrum_along(prod_re, prod_im, icos_y, isin_y, "ijk,jn->ink")
        prod_re, prod_im = spectrum_along(prod_re, prod_im, icos_x, isin_x, "ink,im->mnk")
        real_out = contract("mnk,kz->mnz", prod_re, icos_z) - contract(
            "mnk,kz->mnz", prod_im, isin_z
        )
        return real_out * inverse_scale

    numer = lax.map(correlate, kernels)
    squares = field_in * field_in
    energy = contract(
        "xyz,zn->xyn", squares, band_table(pos_z, jnp.arange(BZ, dtype=jnp.int32), len_z)
    )
    energy = contract(
        "xyn,ym->xmn", energy, band_table(pos_y, jnp.arange(BY, dtype=jnp.int32), len_y)
    )
    energy = contract("xmn,xl->lmn", energy, band_table(pos_x, out_x, len_x))
    scores = numer / jnp.sqrt(energy + epsilon)[None]
    weights = counts.astype(jnp.float32)
    weighted = weights[:, None, None, None] * jnp.exp(sharpness * scores)
    grouped = jnp.sum(weighted.reshape(FIELDS, NT // FIELDS, rows_x, BY, BZ), axis=1)
    totals = jnp.sum(weights.reshape(FIELDS, NT // FIELDS), axis=1)
    fields = jnp.log(grouped / totals[:, None, None, None])
    return fields.reshape(FIELDS, rows_x, BY * BZ)


def solution(mesh):
    in_specs = (P(("grp", "gx"), None), P(None, "gx"), P(), P(), P())
    out_specs = P(None, ("grp", "gx"), None)
    return jax.shard_map(local, mesh=mesh, in_specs=in_specs, out_specs=out_specs, check_vma=False)
```

profile of v0, /device:TPU:0, one launch (start us, length us, event | category | flops | bytes accessed | tf_op | source)
XLA Modules:
  0.0 316.0 jit_solution(17705312637097414959)
XLA Ops:
  0.0 0.8 fusion.433
  0.8 2.3 collective-permute-start
  3.3 1.3 collective-permute-start.1
  4.6 0.7 compare_select_fusion.3
  5.3 0.7 and_select_fusion.8
  6.1 0.8 multiply_reduce_fusion.4
  6.9 25.6 %all_gather.3 = f32[8,4096]{1,0:T(8,128)S(1)} all-gather(f32[8,256]{1,0:T(8,128)} %param.9), channel_id=1, replica_groups=mesh['grp'=2,'gx'=16] {'gx'}, dimensions={1}, use_global_device_ids=true | all-gather | bytes 139264 | tf_op jit(solution)/shard_map/all_gather | solution.py:89
  32.9 0.6 gather_fusion
  33.5 200.1 %gather_fusion.1 = f32[32768]{0:T(1024)S(1)} fusion(f32[8,4096]{1,0:T(8,128)S(1)} %gather_fusion, s32[32768]{0:T(1024)S(1)} %bitcast.250), kind=kCustom, calls=%fused_computation.1 | custom fusion | bytes 524288 | tf_op jit(solution)/shard_map/vmap()/gather | solution.py:52
  235.9 0.6 fusion.332
  236.6 0.6 fusion.336
  237.2 0.6 fusion.250
  237.9 0.6 fusion.254
  239.8 0.6 fusion.249
  240.5 0.6 convolution_subtract_fusion.5
  241.0 0.6 convolution_add_fusion.4
  241.6 73.3 %while.12 = (s32[]{:T(128)}, f32[8,16,8,112]{3,2,1,0:T(8,128)S(1)}, f32[8,4096]{1,0:T(8,128)S(1)}, f32[32,24,128]{2,0,1:T(8,128)S(1)}, f32[32,24,128]{2,0,1:T(8,128)S(1)}, /*index=5*/s32[]{:T(128)}) while((s32[]{:T(128)}, f32[8,16,8,112]{3,2,1,0:T(8,128)S(1)}, f32[8,4096]{1,0:T(8,128)S(1)}, ...), condition=%wide.region_7.8_spmd.clone.clone, body=%wide.region_6.7_spmd.clone.clone.sunk | while | flops 234336256 | bytes 10379349 | solution.py:130
  244.3 0.6 fusion.549
  244.8 0.6 fusion.545
  245.4 0.6 fusion.548
  246.0 0.7 multiply_subtract_fusion.2
  253.4 0.6 fusion.549
  254.0 0.6 fusion.545
  254.6 0.6 fusion.548
  255.1 0.7 multiply_subtract_fusion.2
  262.6 0.6 fusion.549
  263.1 0.6 fusion.545
  263.7 0.6 fusion.548
  264.3 0.7 multiply_subtract_fusion.2
  271.7 0.6 fusion.549
  272.3 0.6 fusion.545
  272.8 0.6 fusion.548
  273.4 0.7 multiply_subtract_fusion.2
  280.8 0.6 fusion.549
  281.4 0.6 fusion.545
  282.0 0.6 fusion.548
  282.5 0.7 multiply_subtract_fusion.2
  290.0 0.6 fusion.549
  290.5 0.6 fusion.545
  291.1 0.6 fusion.548
  291.7 0.7 multiply_subtract_fusion.2
  299.1 0.6 fusion.549
  300.2 0.6 fusion.548
  300.8 0.7 multiply_subtract_fusion.2
  308.2 0.6 fusion.549
  309.4 0.6 fusion.548
  310.0 0.7 multiply_subtract_fusion.2
  315.2 0.8 divide_log_fusion
  (192 shorter events, 58.1 us)
Async XLA Ops:
  0.8 233.9 %collective-permute-start = (f32[8,8,112]{2,1,0:T(8,128)S(1)}, f32[8,8,112]{2,1,0:T(8,128)S(1)}, u32[]{:S(2)}, u32[]{:S(2)}) collective-permute-start(f32[8,8,112]{2,1,0:T(8,128)S(1)} %slice.34), channel_id=1, source_target_pairs={{0,1},{1,2},{2,3},{3,4},{4,5},{5,6},{6,7},{7,8},{8,9},{9,10},{10,1... | collective-permute-start | bytes 86024 | tf_op jit(solution)/shard_map/ppermute | solution.py:28
  3.3 231.5 %collective-permute-start.1 = (f32[8,8,112]{2,1,0:T(8,128)S(1)}, f32[8,8,112]{2,1,0:T(8,128)S(1)}, u32[]{:S(2)}, u32[]{:S(2)}) collective-permute-start(f32[8,8,112]{2,1,0:T(8,128)S(1)} %slice.36), channel_id=1, source_target_pairs={{1,0},{2,1},{3,2},{4,3},{5,4},{6,5},{7,6},{8,7},{9,8},{10,9},{11,1... | collective-permute-start | bytes 86024 | tf_op jit(solution)/shard_map/ppermute | solution.py:29
  233.6 0.8 copy-start
  233.6 0.9 copy-start.1
where the time goes:
time: 316 us
  local copies, waits for them, and re-layouts  203 us (64%)
  matrix products  77.2 us (24%)
  blocking collectives  25.6 us (8%)
  other arithmetic  4.22 us (1%)
  starting transfers between devices  3.63 us (1%)
    gather x2, local copies, waits for them, and re-layouts, rotate_template(): return flat_base[source]  200 us
    dot_general x173, matrix products, contract(): return jnp.einsum(letters, data, table, precision=lax.Precision.HIGHEST)  77.2 us
    all_gather x1, blocking collectives, local(): gathered = lax.all_gather(bank, 'gx', axis=1, tiled=True)  25.6 us
  transfers between devices with their start and end apart: 2, of which 0 were waited for; matrix products, arithmetic and copies ran while one was open for 65% of the time, Pallas kernels for 0%

commit v1 on v0

v1 whole, which is shorter than its diff:
```python
import functools

import jax
import jax.numpy as jnp
from jax import lax
from jax.experimental import pallas as pl
from jax.experimental.pallas import tpu as pltpu
from jax.sharding import PartitionSpec as P

BY = 8
BZ = 112
TS = 16
NT = 8
FIELDS = 4
PER = NT // FIELDS
ROWS = 16
EXT = ROWS + TS
LANES = 128
KB = TS * EXT
HALF = TS // 2
MESH = pl.DeviceIdType.MESH

epsilon = 1e-05
sharpness = 80.0
f32 = jnp.float32
bf16 = jnp.bfloat16


def lane_iota(shape):
    return lax.broadcasted_iota(jnp.int32, shape, len(shape) - 1)


def swap_bit(tiles, bit, dist, lane):
    out = list(tiles)
    low = (lane & dist) == 0
    for i in range(TS):
        if i & (1 << bit):
            continue
        j = i | (1 << bit)
        for h in range(2):
            a, b = tiles[i][h], tiles[j][h]
            na = jnp.where(low, a, pltpu.roll(b, dist, 1))
            nb = jnp.where(low, pltpu.roll(a, LANES - dist, 1), b)
            out[i] = [na if g == h else out[i][g] for g in range(2)]
            out[j] = [nb if g == h else out[j][g] for g in range(2)]
    return out


def swap_high(tiles):
    out = [None] * TS
    for i in range(TS):
        top = i >> 3
        out[i] = [tiles[(i & 7) | (h << 3)][top] for h in range(2)]
    return out


def kernel(n, gather, orient, bank_id, counts, vol, bank, out, sendbuf, slots, ext, pst, wst, hot, lhs, rot,
           bsend, brecv, hsend, hrecv):
    me = lax.axis_index("gx")
    has_left = me > 0
    has_right = me < n - 1
    left = jnp.maximum(me - 1, 0)
    right = jnp.minimum(me + 1, n - 1)

    barrier = pltpu.get_barrier_semaphore()
    if gather:
        for k in range(1, n):
            pl.semaphore_signal(barrier, inc=1, device_id={"gx": lax.rem(me + k, n)}, device_id_type=MESH)
    else:
        @pl.when(has_left)
        def _():
            pl.semaphore_signal(barrier, inc=1, device_id={"gx": left}, device_id_type=MESH)

        @pl.when(has_right)
        def _():
            pl.semaphore_signal(barrier, inc=1, device_id={"gx": right}, device_id_type=MESH)

    if gather:
        for t in range(NT):
            sendbuf[t:t + 1, :] = bank[pl.ds(bank_id[t], 1), :]
        slots[me] = sendbuf[...]
        pl.semaphore_wait(barrier, n - 1)
    else:
        slots[...] = bank[...]

        @pl.when(has_left)
        def _():
            pl.semaphore_wait(barrier, 1)

        @pl.when(has_right)
        def _():
            pl.semaphore_wait(barrier, 1)

    to_right = pltpu.make_async_remote_copy(
        src_ref=vol.at[pl.ds(ROWS - HALF, HALF)], dst_ref=ext.at[pl.ds(0, HALF)],
        send_sem=hsend.at[0], recv_sem=hrecv.at[0], device_id={"gx": right}, device_id_type=MESH)
    to_left = pltpu.make_async_remote_copy(
        src_ref=vol.at[pl.ds(0, HALF)], dst_ref=ext.at[pl.ds(HALF + ROWS, HALF)],
        send_sem=hsend.at[1], recv_sem=hrecv.at[1], device_id={"gx": left}, device_id_type=MESH)

    @pl.when(has_right)
    def _():
        to_right.start()

    @pl.when(has_left)
    def _():
        to_left.start()

    sends = []
    if gather:
        for k in range(1, n):
            copy = pltpu.make_async_remote_copy(
                src_ref=sendbuf, dst_ref=slots.at[me], send_sem=bsend.at[k], recv_sem=brecv.at[k],
                device_id={"gx": lax.rem(me + k, n)}, device_id_type=MESH)
            copy.start()
            sends.append(copy)

    ext[pl.ds(HALF, ROWS), :] = vol[...]

    @pl.when(jnp.logical_not(has_left))
    def _():
        ext[pl.ds(0, HALF), :] = jnp.zeros((HALF, BY * BZ), f32)

    @pl.when(jnp.logical_not(has_right))
    def _():
        ext[pl.ds(HALF + ROWS, HALF), :] = jnp.zeros((HALF, BY * BZ), f32)

    wide = (TS * TS, KB)
    lane = lane_iota((1, KB))
    c_of, a_of = lane >> 5, lane & 31
    row = lax.broadcasted_iota(jnp.int32, wide, 0)
    for g in range(8):
        u = a_of if g & 4 else c_of
        v = c_of if g & 4 else a_of
        u = (TS - 1 - u) if g & 2 else u
        v = (TS - 1 - v) if g & 1 else v
        source = jnp.where(a_of < TS, u * TS + v, -1)
        hot[pl.ds(g * TS * TS, TS * TS), :] = jnp.where(row == source, 1.0, 0.0).astype(bf16)

    @pl.when(has_left)
    def _():
        to_right.wait_recv()

    @pl.when(has_right)
    def _():
        to_left.wait_recv()

    zl = lane_iota((EXT, LANES))
    total = None
    for y in range(BY):
        if y == 0:
            value = ext[:, pl.ds(0, LANES)]
        else:
            value = pltpu.roll(ext[:, pl.ds((y - 1) * LANES, LANES)], TS * y, 1)
            if y < BY - 1:
                value = jnp.where(zl < TS * y, value, pltpu.roll(ext[:, pl.ds(y * LANES, LANES)], TS * y, 1))
        value = jnp.where(zl < BZ, value, 0.0)
        square = value * value
        total = square if total is None else total + square
        for c in range(TS):
            shifted = value if c == HALF else pltpu.roll(value, (HALF - c) % LANES, 1)
            high = shifted.astype(bf16)
            low = (shifted - high.astype(f32)).astype(bf16)
            rows = pl.ds((y * TS + c) * EXT, EXT)
            pst[rows, pl.ds(0, LANES)] = high
            pst[rows, pl.ds(LANES, LANES)] = low
    for step in (1, 2, 4, 8):
        total = total + pltpu.roll(total, LANES - step, 1)
    total = pltpu.roll(total, HALF, 1)
    for step in (1, 2, 4, 8):
        total = total + pltpu.roll(total, EXT - step, 0)
    scale = sharpness * lax.rsqrt(total[:ROWS] + epsilon)

    if gather:
        for k in range(1, n):
            pltpu.make_async_remote_copy(
                src_ref=sendbuf, dst_ref=slots.at[lax.rem(me + n - k, n)], send_sem=bsend.at[k],
                recv_sem=brecv.at[k], device_id={"gx": lax.rem(me + k, n)}, device_id_type=MESH).wait_recv()

    tile = (NT, LANES)
    zero = [[slots[i, :, pl.ds(h * LANES, LANES)] for h in range(2)] for i in range(TS)]
    acc = functools.reduce(jnp.add, [x for pair in zero for x in pair])
    mean = jnp.sum(acc, axis=1, keepdims=True) * (1.0 / TS**3)
    zero = [[x - mean for x in pair] for pair in zero]
    acc = functools.reduce(jnp.add, [x * x for pair in zero for x in pair])
    inv = lax.rsqrt(jnp.sum(acc, axis=1, keepdims=True) + epsilon)
    zero = [[x * inv for x in pair] for pair in zero]

    tl = lane_iota(tile)
    one = swap_high(zero)
    for bit, dist in ((2, 64), (1, 32), (0, 16)):
        one = swap_bit(one, bit, dist, tl)
    two = zero
    for bit, dist in ((3, 8), (2, 4), (1, 2), (0, 1)):
        two = swap_bit(two, bit, dist, tl)

    sub = lax.broadcasted_iota(jnp.int32, tile, 0)
    o = jnp.zeros(tile, jnp.int32)
    for t in range(NT):
        o = jnp.where(sub == t, orient[t], o)
    p = o >> 3
    bit0, bit1, bit2 = o & 1, (o >> 1) & 1, (o >> 2) & 1
    rows0 = (p == 2) | (p == 3)
    rows1 = (p == 0) | (p == 5)
    flip_b = jnp.where(rows0, bit0, jnp.where(rows1, bit1, bit2)) == 1
    flip_u = jnp.where(rows1, bit0, bit1)
    flip_v = jnp.where(rows0 | rows1, bit2, bit0)
    which = (1 - (p & 1)) * 4 + flip_u * 2 + flip_v
    picked = [[jnp.where(rows0, zero[i][h], jnp.where(rows1, one[i][h], two[i][h])) for h in range(2)]
              for i in range(TS)]
    picked = [[jnp.where(flip_b, picked[TS - 1 - i][h], picked[i][h]) for h in range(2)] for i in range(TS)]
    which = jnp.concatenate([which, which], axis=0)
    for i in range(0, TS, 2):
        for h in range(2):
            both = jnp.concatenate([picked[i][h], picked[i + 1][h]], axis=0)
            high = both.astype(bf16).astype(f32)
            low = both - high
            for g in range(8):
                cols = pl.ds(g * TS * TS + h * LANES, LANES)
                lhs[pl.ds(i * NT, 2 * NT), cols] = jnp.where(which == g, high, 0.0).astype(bf16)
                lhs[pl.ds(TS * NT + i * NT, 2 * NT), cols] = jnp.where(which == g, low, 0.0).astype(bf16)
    turned = jnp.dot(lhs[...], hot[...], preferred_element_type=f32)
    rot[...] = turned[:TS * NT] + turned[TS * NT:]

    def band(b, carry):
        for j in range(KB // LANES):
            lines = rot[pl.ds(pl.multiple_of(b * NT, NT), NT), pl.ds(j * LANES, LANES)]
            for t in range(NT):
                line = jnp.broadcast_to(lines[t:t + 1], (ROWS, LANES))
                line = pltpu.roll(line, 0, 1, stride=1, stride_axis=0)
                high = line.astype(bf16)
                low = (line - high.astype(f32)).astype(bf16)
                cols = pl.ds(pl.multiple_of((b - 1) * KB + j * LANES, LANES), LANES)
                wst[pl.ds(t * ROWS, ROWS), cols] = high
                wst[pl.ds((NT + t) * ROWS, ROWS), cols] = low
        return carry

    lax.fori_loop(1, TS, band, 0)

    weights = []
    for k in range(FIELDS):
        parts = [jnp.full((ROWS, LANES), counts[k * PER + i].astype(f32)) for i in range(PER)]
        whole = functools.reduce(jnp.add, parts)
        weights.append([x / whole for x in parts])
    ol = lane_iota((ROWS, LANES))
    half_m = NT * ROWS
    before = [None] * FIELDS
    for y in range(BY):
        res = jnp.dot(wst[:, pl.ds((BY - 1 - y) * KB, BY * KB)], pst[...], preferred_element_type=f32)
        numer = (res[:half_m, :LANES] + (res[:half_m, LANES:] + res[half_m:, :LANES])) + res[half_m:, LANES:]
        for k in range(FIELDS):
            value = None
            for i in range(PER):
                t = k * PER + i
                term = weights[k][i] * jnp.exp(numer[t * ROWS:(t + 1) * ROWS] * scale)
                value = term if value is None else value + term
            value = jnp.log(value)
            if y:
                value = pltpu.roll(value, LANES - TS * y, 1)
                out[k, :, pl.ds((y - 1) * LANES, LANES)] = jnp.where(ol < BZ - TS * (y - 1), before[k], value)
            before[k] = value

    if gather:
        for copy in sends:
            copy.wait_send()

    @pl.when(has_right)
    def _():
        to_right.wait_send()

    @pl.when(has_left)
    def _():
        to_left.wait_send()


def local(n, volume, bank, orient, bank_id, counts):
    gather = bank.shape[1] == TS * TS
    if not gather:
        whole = lax.all_gather(bank, "gx", axis=1, tiled=True)[bank_id]
        bank = whole.reshape(NT, TS, TS * TS).transpose(1, 0, 2)
    smem = pl.BlockSpec(memory_space=pltpu.SMEM)
    vmem = pl.BlockSpec(memory_space=pltpu.VMEM)
    return pl.pallas_call(
        functools.partial(kernel, n, gather),
        out_shape=jax.ShapeDtypeStruct((FIELDS, ROWS, BY * BZ), f32),
        in_specs=[smem, smem, smem, vmem, vmem],
        out_specs=vmem,
        scratch_shapes=[
            pltpu.VMEM((NT, TS * TS), f32),
            pltpu.VMEM((TS, NT, TS * TS), f32),
            pltpu.VMEM((EXT, BY * BZ), f32),
            pltpu.VMEM((BY * KB, 2 * LANES), bf16),
            pltpu.VMEM((2 * NT * ROWS, (TS - 1) * KB), bf16),
            pltpu.VMEM((8 * TS * TS, KB), bf16),
            pltpu.VMEM((2 * TS * NT, 8 * TS * TS), bf16),
            pltpu.VMEM((TS * NT, KB), f32),
            pltpu.SemaphoreType.DMA((TS,)),
            pltpu.SemaphoreType.DMA((TS,)),
            pltpu.SemaphoreType.DMA((2,)),
            pltpu.SemaphoreType.DMA((2,)),
        ],
        compiler_params=pltpu.CompilerParams(
            collective_id=0, has_side_effects=True, vmem_limit_bytes=40 * 1024 * 1024),
        cost_estimate=pl.CostEstimate(flops=4_000_000_000, bytes_accessed=400_000, transcendentals=200_000),
    )(orient, bank_id, counts, volume, bank)


def solution(mesh):
    in_specs = (P(("grp", "gx"), None), P(None, "gx"), P(), P(), P())
    out_specs = P(None, ("grp", "gx"), None)
    return jax.shard_map(functools.partial(local, mesh.shape["gx"]), mesh=mesh, in_specs=in_specs,
                         out_specs=out_specs, check_vma=False)
```

time: 316 us -> 23.2 us (0.07)
  local copies, waits for them, and re-layouts: 203 us -> 4.17 us
  matrix products: 77.2 us -> 0 us
  blocking collectives: 25.6 us -> 0 us
  Pallas kernels: 0 us -> 18.8 us
  other arithmetic: 4.22 us -> 0 us
  starting transfers between devices: 3.63 us -> 0 us
    gather x3 -> x0, local copies, waits for them, and re-layouts: 201 us -> none  [the longest x2 200 us: rotate_template(): return flat_base[source]]
    dot_general x173 -> x0, matrix products: 77.2 us -> none  [contract(): return jnp.einsum(letters, data, table, precision=lax.Precision.HIGHEST)]
    all_gather x1 -> x0, blocking collectives: 25.6 us -> none  [local(): gathered = lax.all_gather(bank, 'gx', axis=1, tiled=True)]
    pallas_call x0 -> x1, Pallas kernels: none -> 18.8 us  [local(): pl.pallas_call(functools.partial(kernel, n, gather), out_shape=jax.ShapeD...]
    unnamed x7 -> x11, local copies, waits for them, and re-layouts: 0.32 us -> 4.17 us
    ppermute x2 -> x0, starting transfers between devices: 3.63 us -> none  [the longest x1 2.35 us: extended(): before = lax.ppermute(last, axis, up)]
  transfers between devices with their start and end apart: 2 -> 0, of which waited for: 0 -> 0; matrix products, arithmetic and copies ran while one was open for 65% -> 0% of each run, Pallas kernels for 0% -> 0%
where the time goes in v1:
time: 23.2 us; the launch traced here: 23 us
  Pallas kernels  18.8 us (81%)
  local copies, waits for them, and re-layouts  4.17 us (18%)
    pallas_call x1, Pallas kernels, local(): pl.pallas_call(functools.partial(kernel, n, gather), out_shape=jax.ShapeD...  18.8 us
    unnamed x11, local copies, waits for them, and re-layouts  4.17 us

profile of v1, /device:TPU:0, one launch (start us, length us, event | category | flops | bytes accessed | tf_op | source)
XLA Modules:
  0.0 23.0 jit_solution(15678593388263743168)
XLA Ops:
  0.0 0.0 copy-start
  0.0 0.8 %copy-done = f32[16,896]{1,0:T(8,128)S(1)} copy-done((f32[16,896]{1,0:T(8,128)S(1)}, f32[16,896]{1,0:T(8,128)}, u32[]{:S(2)}) %copy-start) | copy-done | bytes 57368
  0.8 0.0 copy-start.1
  0.8 0.7 %copy-done.1 = f32[8,256]{1,0:T(8,128)S(1)} copy-done((f32[8,256]{1,0:T(8,128)S(1)}, f32[8,256]{1,0:T(8,128)}, u32[]{:S(2)}) %copy-start.1) | copy-done | bytes 8216
  1.5 0.0 copy-start.2
  1.5 0.7 %copy-done.2 = s32[8]{0:T(128)S(1)} copy-done((s32[8]{0:T(128)S(1)}, s32[8]{0:T(128)}, u32[]{:S(2)}) %copy-start.2) | copy-done | bytes 56
  2.2 0.0 copy-start.3
  2.2 0.7 %copy-done.3 = s32[8]{0:T(128)S(1)} copy-done((s32[8]{0:T(128)S(1)}, s32[8]{0:T(128)}, u32[]{:S(2)}) %copy-start.3) | copy-done | bytes 56
  2.8 0.0 copy-start.4
  2.8 0.7 %copy-done.4 = s32[8]{0:T(128)S(1)} copy-done((s32[8]{0:T(128)S(1)}, s32[8]{0:T(128)}, u32[]{:S(2)}) %copy-start.4) | copy-done | bytes 56
  3.5 18.8 %shard_map.55 = f32[4,16,896]{2,1,0:T(8,128)S(1)} custom-call(s32[8]{0:T(128)S(1)} %copy-done.2, s32[8]{0:T(128)S(1)} %copy-done.3, s32[8]{0:T(128)S(1)} %copy-done.4, f32[16,896]{1,0:T(8,128)S(1)} %copy-done, f32[8,256]{1,0:T(8,128)S(1)} %copy-done.1), custom_call_target="tpu_custom_call" | custom-call | flops 4000000000 | bytes 400000 | tf_op jit(solution)/shard_map/pallas_call | solution.py:283
  22.3 0.7 %copy.7 = f32[4,16,896]{2,1,0:T(8,128)} copy(f32[4,16,896]{2,1,0:T(8,128)S(1)} %shard_map.55) | data formatting | bytes 458752
Async XLA Ops:
  0.0 0.8 %copy-start = (f32[16,896]{1,0:T(8,128)S(1)}, f32[16,896]{1,0:T(8,128)}, u32[]{:S(2)}) copy-start(f32[16,896]{1,0:T(8,128)} %vol.1) | copy-start | bytes 172036
  0.8 0.7 %copy-start.1 = (f32[8,256]{1,0:T(8,128)S(1)}, f32[8,256]{1,0:T(8,128)}, u32[]{:S(2)}) copy-start(f32[8,256]{1,0:T(8,128)} %bank.1) | copy-start | bytes 24580
  1.5 0.7 %copy-start.2 = (s32[8]{0:T(128)S(1)}, s32[8]{0:T(128)}, u32[]{:S(2)}) copy-start(s32[8]{0:T(128)} %orient.1) | copy-start | bytes 100
  2.2 0.7 %copy-start.3 = (s32[8]{0:T(128)S(1)}, s32[8]{0:T(128)}, u32[]{:S(2)}) copy-start(s32[8]{0:T(128)} %bank_id.1) | copy-start | bytes 100
  2.8 0.7 %copy-start.4 = (s32[8]{0:T(128)S(1)}, s32[8]{0:T(128)}, u32[]{:S(2)}) copy-start(s32[8]{0:T(128)} %counts.1) | copy-start | bytes 100

commit v2 on v1

--- a/solution.py
+++ b/solution.py
@@ -54,8 +54,12 @@
     return out
 
 
-def kernel(n, gather, orient, bank_id, counts, vol, bank, out, sendbuf, slots, ext, pst, wst, hot, lhs, rot,
-           bsend, brecv, hsend, hrecv):
+def kernel(n, gather, orient_in, bank_id_in, counts_in, vol_in, bank_in, out, orient, bank_id, counts, vol, bank,
+           sendbuf, slots, ext, pst, wst, hot, lhs, rot, fetch, bsend, brecv, hsend, hrecv):
+    pairs = ((vol_in, vol), (bank_id_in, bank_id), (bank_in, bank), (orient_in, orient), (counts_in, counts))
+    fetches = [pltpu.make_async_copy(src, dst, fetch.at[i]) for i, (src, dst) in enumerate(pairs)]
+    for copy in fetches:
+        copy.start()
     me = lax.axis_index("gx")
     has_left = me > 0
     has_right = me < n - 1
@@ -75,6 +79,8 @@
         def _():
             pl.semaphore_signal(barrier, inc=1, device_id={"gx": right}, device_id_type=MESH)
 
+    for copy in fetches:
+        copy.wait()
     if gather:
         for t in range(NT):
             sendbuf[t:t + 1, :] = bank[pl.ds(bank_id[t], 1), :]
@@ -224,18 +230,20 @@
 
     def band(b, carry):
         for j in range(KB // LANES):
-            lines = rot[pl.ds(pl.multiple_of(b * NT, NT), NT), pl.ds(j * LANES, LANES)]
+            first = b * NT if isinstance(b, int) else pl.multiple_of(b * NT, NT)
+            lines = rot[pl.ds(first, NT), pl.ds(j * LANES, LANES)]
             for t in range(NT):
                 line = jnp.broadcast_to(lines[t:t + 1], (ROWS, LANES))
                 line = pltpu.roll(line, 0, 1, stride=1, stride_axis=0)
                 high = line.astype(bf16)
                 low = (line - high.astype(f32)).astype(bf16)
-                cols = pl.ds(pl.multiple_of((b - 1) * KB + j * LANES, LANES), LANES)
+                start = (b - 1) * KB + j * LANES
+                cols = pl.ds(start if isinstance(b, int) else pl.multiple_of(start, LANES), LANES)
                 wst[pl.ds(t * ROWS, ROWS), cols] = high
                 wst[pl.ds((NT + t) * ROWS, ROWS), cols] = low
         return carry
 
-    lax.fori_loop(1, TS, band, 0)
+    lax.fori_loop(1, BY + 1, band, 0)
 
     weights = []
     for k in range(FIELDS):
@@ -244,8 +252,10 @@
         weights.append([x / whole for x in parts])
     ol = lane_iota((ROWS, LANES))
     half_m = NT * ROWS
-    before = [None] * FIELDS
-    for y in range(BY):
+    after = [None] * FIELDS
+    for y in reversed(range(BY)):
+        if y:
+            band(TS - y, 0)
         res = jnp.dot(wst[:, pl.ds((BY - 1 - y) * KB, BY * KB)], pst[...], preferred_element_type=f32)
         numer = (res[:half_m, :LANES] + (res[:half_m, LANES:] + res[half_m:, :LANES])) + res[half_m:, LANES:]
         for k in range(FIELDS):
@@ -257,8 +267,9 @@
             value = jnp.log(value)
             if y:
                 value = pltpu.roll(value, LANES - TS * y, 1)
-                out[k, :, pl.ds((y - 1) * LANES, LANES)] = jnp.where(ol < BZ - TS * (y - 1), before[k], value)
-            before[k] = value
+            if y < BY - 1:
+                out[k, :, pl.ds(y * LANES, LANES)] = jnp.where(ol < BZ - TS * y, value, after[k])
+            after[k] = value
 
     if gather:
         for copy in sends:
@@ -278,14 +289,19 @@
     if not gather:
         whole = lax.all_gather(bank, "gx", axis=1, tiled=True)[bank_id]
         bank = whole.reshape(NT, TS, TS * TS).transpose(1, 0, 2)
-    smem = pl.BlockSpec(memory_space=pltpu.SMEM)
+    hbm = pl.BlockSpec(memory_space=pltpu.HBM)
     vmem = pl.BlockSpec(memory_space=pltpu.VMEM)
     return pl.pallas_call(
         functools.partial(kernel, n, gather),
         out_shape=jax.ShapeDtypeStruct((FIELDS, ROWS, BY * BZ), f32),
-        in_specs=[smem, smem, smem, vmem, vmem],
+        in_specs=[hbm] * 5,
         out_specs=vmem,
         scratch_shapes=[
+            pltpu.SMEM((NT,), jnp.int32),
+            pltpu.SMEM((NT,), jnp.int32),
+            pltpu.SMEM((NT,), jnp.int32),
+            pltpu.VMEM(volume.shape, f32),
+            pltpu.VMEM(bank.shape, f32),
             pltpu.VMEM((NT, TS * TS), f32),
             pltpu.VMEM((TS, NT, TS * TS), f32),
             pltpu.VMEM((EXT, BY * BZ), f32),
@@ -294,13 +310,14 @@
             pltpu.VMEM((8 * TS * TS, KB), bf16),
             pltpu.VMEM((2 * TS * NT, 8 * TS * TS), bf16),
             pltpu.VMEM((TS * NT, KB), f32),
+            pltpu.SemaphoreType.DMA((5,)),
             pltpu.SemaphoreType.DMA((TS,)),
             pltpu.SemaphoreType.DMA((TS,)),
             pltpu.SemaphoreType.DMA((2,)),
             pltpu.SemaphoreType.DMA((2,)),
         ],
         compiler_params=pltpu.CompilerParams(
-            collective_id=0, has_side_effects=True, vmem_limit_bytes=40 * 1024 * 1024),
+            collective_id=0, has_side_effects=True, vmem_limit_bytes=64 * 1024 * 1024),
         cost_estimate=pl.CostEstimate(flops=4_000_000_000, bytes_accessed=400_000, transcendentals=200_000),
     )(orient, bank_id, counts, volume, bank)
 

time: 23.2 us -> 19.8 us (0.85)
  local copies, waits for them, and re-layouts: 4.17 us -> 1.64 us
  Pallas kernels: 18.8 us -> 17.9 us
    unnamed x11 -> x1, local copies, waits for them, and re-layouts: 4.17 us -> 1.64 us
    pallas_call x1, Pallas kernels: 18.8 us -> 17.9 us  [local(): pl.pallas_call(functools.partial(kernel, n, gather), out_shape=jax.ShapeD...]
where the time goes in v2:
time: 19.8 us; the launch traced here: 19.6 us
  Pallas kernels  17.9 us (90%)
  local copies, waits for them, and re-layouts  1.64 us (8%)
    pallas_call x1, Pallas kernels, local(): pl.pallas_call(functools.partial(kernel, n, gather), out_shape=jax.ShapeD...  17.9 us
    unnamed x1, local copies, waits for them, and re-layouts  1.64 us

profile of v2, /device:TPU:0, one launch (start us, length us, event | category | flops | bytes accessed | tf_op | source)
XLA Modules:
  0.0 19.6 jit_solution(17902596192529722251)
XLA Ops:
  0.0 17.9 %shard_map.55 = f32[4,16,896]{2,1,0:T(8,128)} custom-call(s32[8]{0:T(128)} %orient_in.1, s32[8]{0:T(128)} %bank_id_in.1, s32[8]{0:T(128)} %counts_in.1, f32[16,896]{1,0:T(8,128)} %vol_in.1, f32[8,256]{1,0:T(8,128)} %bank_in.1), custom_call_target="tpu_custom_call" | custom-call | flops 4000000000 | bytes 400000 | tf_op jit(solution)/shard_map/pallas_call | solution.py:294
  17.9 1.6 %copy.7 = f32[4,16,896]{2,1,0:T(8,128)} copy(f32[4,16,896]{2,1,0:T(8,128)} %shard_map.55) | data formatting | bytes 458752

commit v3 on v2

--- a/solution.py
+++ b/solution.py
@@ -79,8 +79,8 @@
         def _():
             pl.semaphore_signal(barrier, inc=1, device_id={"gx": right}, device_id_type=MESH)
 
-    for copy in fetches:
-        copy.wait()
+    fetches[1].wait()
+    fetches[2].wait()
     if gather:
         for t in range(NT):
             sendbuf[t:t + 1, :] = bank[pl.ds(bank_id[t], 1), :]
@@ -104,23 +104,27 @@
         src_ref=vol.at[pl.ds(0, HALF)], dst_ref=ext.at[pl.ds(HALF + ROWS, HALF)],
         send_sem=hsend.at[1], recv_sem=hrecv.at[1], device_id={"gx": left}, device_id_type=MESH)
 
-    @pl.when(has_right)
-    def _():
-        to_right.start()
-
-    @pl.when(has_left)
-    def _():
-        to_left.start()
-
     sends = []
     if gather:
-        for k in range(1, n):
+        for k in sorted(range(1, n), key=lambda i: -min(i, n - i)):
             copy = pltpu.make_async_remote_copy(
                 src_ref=sendbuf, dst_ref=slots.at[me], send_sem=bsend.at[k], recv_sem=brecv.at[k],
                 device_id={"gx": lax.rem(me + k, n)}, device_id_type=MESH)
             copy.start()
             sends.append(copy)
 
+    fetches[0].wait()
+
+    @pl.when(has_right)
+    def _():
+        to_right.start()
+
+    @pl.when(has_left)
+    def _():
+        to_left.start()
+
+    fetches[3].wait()
+    fetches[4].wait()
     ext[pl.ds(HALF, ROWS), :] = vol[...]
 
     @pl.when(jnp.logical_not(has_left))

time: 19.8 us -> 19.7 us (level)
  no operation moved by 1% of the time
where the time goes in v3:
time: 19.7 us; the launch traced here: 19.5 us
  Pallas kernels  17.9 us (91%)
  local copies, waits for them, and re-layouts  1.64 us (8%)
    pallas_call x1, Pallas kernels, local(): pl.pallas_call(functools.partial(kernel, n, gather), out_shape=jax.ShapeD...  17.9 us
    unnamed x1, local copies, waits for them, and re-layouts  1.64 us

profile of v3, /device:TPU:0, one launch (start us, length us, event | category | flops | bytes accessed | tf_op | source)
XLA Modules:
  0.0 19.5 jit_solution(10566385839106005728)
XLA Ops:
  0.0 17.9 %shard_map.55 = f32[4,16,896]{2,1,0:T(8,128)} custom-call(s32[8]{0:T(128)} %orient_in.1, s32[8]{0:T(128)} %bank_id_in.1, s32[8]{0:T(128)} %counts_in.1, f32[16,896]{1,0:T(8,128)} %vol_in.1, f32[8,256]{1,0:T(8,128)} %bank_in.1), custom_call_target="tpu_custom_call" | custom-call | flops 4000000000 | bytes 400000 | tf_op jit(solution)/shard_map/pallas_call | solution.py:298
  17.9 1.6 %copy.7 = f32[4,16,896]{2,1,0:T(8,128)} copy(f32[4,16,896]{2,1,0:T(8,128)} %shard_map.55) | data formatting | bytes 458752

commit v4 on v3

--- a/solution.py
+++ b/solution.py
@@ -247,7 +247,8 @@
                 wst[pl.ds((NT + t) * ROWS, ROWS), cols] = low
         return carry
 
-    lax.fori_loop(1, BY + 1, band, 0)
+    for b in range(1, BY + 1):
+        band(b, 0)
 
     weights = []
     for k in range(FIELDS):

time: 19.7 us -> 18.7 us (0.949)
  Pallas kernels: 17.9 us -> 16.8 us
    pallas_call x1, Pallas kernels: 17.9 us -> 16.8 us  [local(): pl.pallas_call(functools.partial(kernel, n, gather), out_shape=jax.ShapeD...]
where the time goes in v4:
time: 18.7 us; the launch traced here: 18.5 us
  Pallas kernels  16.8 us (90%)
  local copies, waits for them, and re-layouts  1.64 us (9%)
    pallas_call x1, Pallas kernels, local(): pl.pallas_call(functools.partial(kernel, n, gather), out_shape=jax.ShapeD...  16.8 us
    unnamed x1, local copies, waits for them, and re-layouts  1.64 us

profile of v4, /device:TPU:0, one launch (start us, length us, event | category | flops | bytes accessed | tf_op | source)
XLA Modules:
  0.0 18.5 jit_solution(660083540720036109)
XLA Ops:
  0.0 16.8 %shard_map.55 = f32[4,16,896]{2,1,0:T(8,128)} custom-call(s32[8]{0:T(128)} %orient_in.1, s32[8]{0:T(128)} %bank_id_in.1, s32[8]{0:T(128)} %counts_in.1, f32[16,896]{1,0:T(8,128)} %vol_in.1, f32[8,256]{1,0:T(8,128)} %bank_in.1), custom_call_target="tpu_custom_call" | custom-call | flops 4000000000 | bytes 400000 | tf_op jit(solution)/shard_map/pallas_call | solution.py:299
  16.8 1.6 %copy.7 = f32[4,16,896]{2,1,0:T(8,128)} copy(f32[4,16,896]{2,1,0:T(8,128)} %shard_map.55) | data formatting | bytes 458752
